TPU v7x, 512 devices: a whole 4x4x16 slice. The times are simulated.
512 devices in a mesh: dp: 64 (over z_hi, x, y, core), section: 8 (over z_lo).
Axes of the slice: x: 4, y: 4, z: 16 (z_hi: 2, z_lo: 8; z = z_hi * 8 + z_lo), core: 2. Of those that a mesh axis runs over, the one named last changes fastest.
Arguments:
- projections: float32 [2048, 128], P('dp'), may hold values from -2.5 to 2.5
- partner: int32 [2048], P('dp'), may hold values from 0 to 2047, as said below
- plan: int32 [64, 32], P('dp'), may hold values from 0 to 31, as said below
- head_pre: bfloat16 [128, 2048], P('dp', 'section'), may hold values from -6 to 6
- head_in: bfloat16 [512, 2048], P(None, 'section'), may hold values from -0.25 to 0.25
- head_out: bfloat16 [2048, 128], P('section'), may hold values from -0.125 to 0.125
- final_pre: bfloat16 [128, 8, 8, 8, 512], P('dp'), may hold values from -6 to 6
- incoming: bfloat16 [8, 128, 8, 8, 8, 512], P('section', 'dp'), may hold values from -6 to 6
- input_pre: bfloat16 [8, 128, 8, 8, 8, 512], P('section', 'dp'), may hold values from -6 to 6
- mid_pre1: bfloat16 [8, 128, 8, 8, 8, 128], P('section', 'dp'), may hold values from -6 to 6
- mid_pre2: bfloat16 [8, 128, 8, 8, 8, 128], P('section', 'dp'), may hold values from -6 to 6
- w_reduce: bfloat16 [8, 512, 128], P('section', 'dp'), may hold values from -0.25 to 0.25
- w_spatial: bfloat16 [8, 3456, 128], P('section', 'dp'), may hold values from -0.109375 to 0.109375
- w_expand: bfloat16 [8, 128, 512], P('section', 'dp'), may hold values from -0.5 to 0.5
- gain1: float32 [8, 128], P('section'), may hold values from 0.5 to 2
- gain2: float32 [8, 128], P('section'), may hold values from 0.5 to 2
- gain3: float32 [8, 512], P('section'), may hold values from 0.5 to 2
Outputs:
- projection_gradient: float32 [2048, 128], P('dp')
- input_grad: bfloat16 [8, 128, 8, 8, 8, 512], P('section', 'dp')
- grad_reduce: bfloat16 [8, 512, 128], P('section', 'dp')
- grad_spatial: bfloat16 [8, 3456, 128], P('section', 'dp')
- grad_expand: bfloat16 [8, 128, 512], P('section', 'dp')
Inputs may be any that keep to these rules, and one draw needn't show every extreme that they name: partner[partner[i]] = i and partner[i] != i for every crop i. `plan`: each row names every number 0 to 31 once; the window's microbatch uses the first 2 entries of each row.
All inputs are finite; a program needn't handle non-finite values.
Results may differ from a plain program's by a relative error of at most 0.009.
Values may be sent and summed in bfloat16 or wider, within the bound.
No kernel may reach another device: no remote copies, remote signals or barrier semaphores. Data moves between devices by JAX's collectives and lax.ppermute only.
A program may use at most 64 MiB of HBM per device.

v0:
```python
import functools

import jax
import jax.numpy as jnp
from jax import lax
from jax.experimental import pallas as pl
from jax.experimental.pallas import tpu as pltpu
from jax.sharding import Mesh
from jax.sharding import PartitionSpec as P

MICRO = 2
SOFTMAX_TEMP = 0.5
LOSS_SCALE = 1024.0
PLANE = ("x", "y", "core")
DP = ("z_hi", "x", "y", "core")
LANES = 128
TILE = 256
BF = jnp.bfloat16
F32 = jnp.float32
ROWS_BY_ROWS = (((1,), (1,)), ((), ()))
VMEM_LIMIT = 24 * 1024 * 1024


def three_parts(values):
    high = values.astype(BF)
    rest = values - high.astype(F32)
    middle = rest.astype(BF)
    return high, middle, (rest - middle.astype(F32)).astype(BF)


def prepare_kernel(
    where_ref,
    final_hbm,
    incoming_hbm,
    mid1_hbm,
    mid2_hbm,
    input_hbm,
    one_hbm,
    two_ref,
    in_hbm,
    base_ref,
    final_ref,
    mid1_ref,
    mid2_ref,
    input_ref,
    one_ref,
    in_ref,
    read_sems,
    write_sems,
):
    rows, narrow = mid1_ref.shape
    wide = input_ref.shape[1]
    crop_rows = rows // MICRO
    reads = [
        pltpu.make_async_copy(source, target, read_sems.at[place])
        for place, (source, target) in enumerate(
            ((mid1_hbm, mid1_ref), (mid2_hbm, mid2_ref), (input_hbm, input_ref))
        )
    ]
    for read in reads:
        read.start()
    write_one = pltpu.make_async_copy(one_ref, one_hbm, write_sems.at[0])
    write_in = pltpu.make_async_copy(in_ref, in_hbm, write_sems.at[1])
    empty = jnp.zeros((64, narrow), BF)
    reads[0].wait()
    for crop in range(MICRO):
        at = slice(crop * crop_rows, (crop + 1) * crop_rows)
        hidden = jnp.maximum(mid1_ref[at, :], 0)
        moved = (
            jnp.concatenate([empty, hidden[:-64]], axis=0),
            hidden,
            jnp.concatenate([hidden[64:], empty], axis=0),
        )
        for off_a in range(3):
            one_ref[off_a * narrow : (off_a + 1) * narrow, at] = moved[off_a].T
    write_one.start()
    reads[1].wait()
    two_ref[...] = jnp.maximum(mid2_ref[...], 0).T
    reads[2].wait()
    for part in range(wide // LANES):
        lanes = slice(part * LANES, (part + 1) * LANES)
        in_ref[lanes, :] = jnp.maximum(input_ref[:, lanes], 0).T
    write_in.start()

    @pl.when(where_ref[0] != 0)
    def _():
        read = pltpu.make_async_copy(final_hbm, final_ref, read_sems.at[3])
        read.start()
        read.wait()
        base_ref[...] = jnp.where(final_ref[...].astype(F32) > 0, 1.0, 0.0).astype(BF)

    @pl.when(where_ref[0] == 0)
    def _():
        read = pltpu.make_async_copy(incoming_hbm, base_ref, read_sems.at[3])
        read.start()
        read.wait()

    write_one.wait()
    write_in.wait()


def prepare_step(place, final, incoming, mid1, mid2, input_pre):
    rows, narrow = mid1.shape
    wide = input_pre.shape[1]
    smem = pl.BlockSpec(memory_space=pltpu.SMEM)
    hbm = pl.BlockSpec(memory_space=pltpu.HBM)
    vmem = pl.BlockSpec(memory_space=pltpu.VMEM)
    held = (final.shape, mid1.shape, mid2.shape, input_pre.shape)
    turned = ((3 * narrow, rows), (wide, rows))
    return pl.pallas_call(
        prepare_kernel,
        out_shape=(
            pltpu.HBM(turned[0], BF),
            pltpu.VMEM((narrow, rows), BF),
            pltpu.HBM(turned[1], BF),
            pltpu.VMEM((rows, wide), BF),
        ),
        in_specs=[smem] + [hbm] * 5,
        out_specs=(hbm, vmem, hbm, vmem),
        scratch_shapes=[pltpu.VMEM(shape, BF) for shape in (*held, *turned)]
        + [pltpu.SemaphoreType.DMA((4,)), pltpu.SemaphoreType.DMA((2,))],
        compiler_params=pltpu.CompilerParams(vmem_limit_bytes=VMEM_LIMIT),
        cost_estimate=pl.CostEstimate(flops=0, bytes_accessed=6_000_000, transcendentals=0),
        name="prepare",
    )(place, *in_hbm(final, incoming, mid1, mid2, input_pre))


def unpack_kernel(
    where_ref,
    near_ref,
    across_ref,
    spatial_ref,
    expand_ref,
    reduce_ref,
    spatial_rows,
    expand_rows,
    reduce_rows,
):
    narrow = near_ref.shape[1]
    chips = near_ref.shape[0] // 144

    def unpack(source, chip, core):
        shard = source[chip * 144 : (chip + 1) * 144, :].astype(F32)
        for half in range(2):
            device = half * 2 * chips + chip * 2 + core
            top = half * 72
            reduce_rows[device * 8 : device * 8 + 8, :] = shard[top : top + 8]
            for part in range(8):
                row, lane = device * 2 + part // 4, part % 4 * LANES
                expand_rows[row : row + 1, lane : lane + LANES] = shard[
                    top + 8 + part : top + 9 + part
                ]
            spatial_rows[device * 54 : device * 54 + 54, :] = shard[top + 16 : top + 70]

    for core in range(2):

        @pl.when(where_ref[1] == core)
        def _(core=core):
            for chip in range(chips):
                unpack(near_ref, chip, core)
                unpack(across_ref, chip, 1 - core)

    reduce_ref[...] = reduce_rows[...].astype(BF)
    expand_ref[...] = expand_rows[...].astype(BF)
    for off_a in range(3):
        for position in range(9):
            block = off_a * 9 + position
            spatial_ref[
                off_a * narrow : (off_a + 1) * narrow, position * narrow : (position + 1) * narrow
            ] = spatial_rows[block * narrow : (block + 1) * narrow, :].astype(BF)


def unpack_step(place, near, across, wide):
    narrow = near.shape[1]
    smem = pl.BlockSpec(memory_space=pltpu.SMEM)
    vmem = pl.BlockSpec(memory_space=pltpu.VMEM)
    outs = ((3 * narrow, 9 * narrow), (narrow, wide), (wide, narrow))
    return pl.pallas_call(
        unpack_kernel,
        out_shape=(
            pltpu.VMEM(outs[0], BF),
            pltpu.VMEM(outs[1], BF),
            jax.ShapeDtypeStruct(outs[2], BF),
        ),
        in_specs=[smem] + [vmem] * 2,
        out_specs=(vmem,) * 3,
        scratch_shapes=[
            pltpu.VMEM((27 * narrow, narrow), F32),
            pltpu.VMEM((narrow, wide), F32),
            pltpu.VMEM((wide, narrow), F32),
        ],
        compiler_params=pltpu.CompilerParams(vmem_limit_bytes=VMEM_LIMIT),
        cost_estimate=pl.CostEstimate(flops=0, bytes_accessed=3_000_000, transcendentals=0),
        name="unpack",
    )(place, *in_vmem(near, across))


def loss_kernel(
    where_ref,
    plan_ref,
    near_ref,
    across_ref,
    partner_ref,
    head_pre_ref,
    head_in_ref,
    head_out_ref,
    grad_ref,
    pool_ref,
    left,
    right,
    even,
    odd,
    totals,
):
    crops = left.shape[0]
    own = grad_ref.shape[0]
    tiles = crops // TILE
    first = pl.multiple_of(where_ref[0], own)

    for half, rows_ref in enumerate((near_ref, across_ref)):
        count = rows_ref.shape[0]

        def split(r, _, half=half, rows_ref=rows_ref, count=count):
            a, b, c = three_parts(rows_ref[pl.ds(pl.multiple_of(r * TILE, TILE), TILE), :])
            at = pl.ds(pl.multiple_of(half * count + r * TILE, TILE), TILE)
            a2, b2, c2 = a * 2, b * 2, c * 2
            for place, part in enumerate((a2, b2, a2, b2, a2, c2)):
                left[at, place * LANES : (place + 1) * LANES] = part
            for place, part in enumerate((a, a, b, b, c, a)):
                right[at, place * LANES : (place + 1) * LANES] = part
            return 0

        lax.fori_loop(0, count // TILE, split, 0)

    diagonal = lax.broadcasted_iota(jnp.int32, (TILE, TILE), 0) == lax.broadcasted_iota(
        jnp.int32, (TILE, TILE), 1
    )
    groups = crops // 8

    def score_block(j, scores):
        at = pl.ds(pl.multiple_of(j * TILE, TILE), TILE)
        scores[...] = lax.dot_general(
            left[...], right[at, :], ROWS_BY_ROWS, preferred_element_type=F32
        )
        scores[at, :] = jnp.where(diagonal, -jnp.inf, scores[at, :])
        largest = jnp.max(scores[...].reshape(groups, 8, TILE), axis=0)
        return jnp.broadcast_to(jnp.max(largest, axis=0, keepdims=True), (8, TILE))

    def sum_block(j, scores, largest):
        at = pl.ds(pl.multiple_of(j * TILE, TILE), TILE)
        summed = jnp.sum(jnp.exp(scores[...].reshape(groups, 8, TILE) - largest[None]), axis=0)
        whole = jnp.broadcast_to(jnp.sum(summed, axis=0, keepdims=True), (8, TILE))
        totals[:, at] = largest + jnp.log(whole)

    def two_blocks(pair, largest):
        j = 2 * pair
        following = score_block(j + 1, odd)
        sum_block(j, even, largest)
        after = score_block(j + 2, even)
        sum_block(j + 1, odd, following)
        return after

    largest = lax.fori_loop(0, tiles // 2 - 1, two_blocks, score_block(0, even))
    following = score_block(tiles - 1, odd)
    sum_block(tiles - 2, even, largest)
    sum_block(tiles - 1, odd, following)

    mine = lax.dot_general(
        left[pl.ds(first, own), :], right[...], ROWS_BY_ROWS, preferred_element_type=F32
    )
    columns = lax.broadcasted_iota(jnp.int32, (own, crops), 1)
    mine = jnp.where(
        columns == lax.broadcasted_iota(jnp.int32, (own, crops), 0) + first, -jnp.inf, mine
    )
    peak = jnp.max(mine, axis=1, keepdims=True)
    my_totals = peak + jnp.log(jnp.sum(jnp.exp(mine - peak), axis=1, keepdims=True))
    blended = jnp.exp(mine - my_totals) + jnp.exp(mine - totals[0:1, :])
    blended = blended - jnp.where(columns == partner_ref[...], 2.0, 0.0)
    a, b, c = three_parts(blended)
    stacked = jnp.concatenate([a, b, c], axis=0)
    products = jnp.dot(stacked, right[:, LANES : 3 * LANES], preferred_element_type=F32)
    low = jnp.dot(a, right[:, 4 * LANES : 5 * LANES], preferred_element_type=F32)
    small = products[own : 2 * own, LANES:] + products[2 * own :, :LANES] + low
    gradient = (
        products[:own, :LANES] + (products[:own, LANES:] + products[own : 2 * own, :LANES] + small)
    ) / SOFTMAX_TEMP
    grad_ref[...] = gradient

    pick_row = lax.broadcasted_iota(jnp.int32, (16, own), 0)
    pick_column = lax.broadcasted_iota(jnp.int32, (16, own), 1)
    wanted = jnp.where(pick_row == 0, plan_ref[0, 0], plan_ref[0, 1])
    chosen = jnp.where((pick_column == wanted) & (pick_row < MICRO), 1.0, 0.0).astype(BF)
    picked = jnp.dot(chosen, gradient.astype(BF), preferred_element_type=F32).astype(BF)
    hid_back = lax.dot_general(
        picked, head_out_ref[...], ROWS_BY_ROWS, preferred_element_type=F32
    )
    hid_grad = jnp.where(head_pre_ref[...].astype(F32) > 0, hid_back[:MICRO], 0.0)
    hid_grad = jnp.concatenate(
        [hid_grad, jnp.zeros((16 - MICRO, hid_grad.shape[1]), F32)], axis=0
    ).astype(BF)
    pool = lax.dot_general(hid_grad, head_in_ref[...], ROWS_BY_ROWS, preferred_element_type=F32)
    parts = pool.shape[1] // LANES
    packed = jnp.concatenate(
        [pool[m : m + 1, n * LANES : (n + 1) * LANES] for m in range(MICRO) for n in range(parts)],
        axis=0,
    )
    for copy in range(pool_ref.shape[0] // packed.shape[0]):
        pool_ref[copy * packed.shape[0] : (copy + 1) * packed.shape[0], :] = packed


def loss_step(first_row, plan, near, across, partner_row, head_pre, head_in, head_out, own, sections):
    crops, width = 2 * near.shape[0], near.shape[1]
    pool_rows = MICRO * head_in.shape[0] // LANES
    smem = pl.BlockSpec(memory_space=pltpu.SMEM)
    vmem = pl.BlockSpec(memory_space=pltpu.VMEM)
    return pl.pallas_call(
        loss_kernel,
        out_shape=(
            jax.ShapeDtypeStruct((own, width), F32),
            jax.ShapeDtypeStruct((sections * pool_rows, LANES), F32),
        ),
        in_specs=[smem, smem] + [vmem] * 6,
        out_specs=(vmem, vmem),
        scratch_shapes=[
            pltpu.VMEM((crops, 6 * LANES), BF),
            pltpu.VMEM((crops, 6 * LANES), BF),
            pltpu.VMEM((crops, TILE), F32),
            pltpu.VMEM((crops, TILE), F32),
            pltpu.VMEM((8, crops), F32),
        ],
        compiler_params=pltpu.CompilerParams(vmem_limit_bytes=VMEM_LIMIT),
        cost_estimate=pl.CostEstimate(
            flops=12_000_000_000, bytes_accessed=2_000_000, transcendentals=4_000_000
        ),
        name="loss",
    )(first_row, plan, *in_vmem(near, across), partner_row, head_pre, head_in, head_out)


def pooled_scale(last, pool_ref, voxels):
    rows = MICRO * 4
    total = pool_ref[0:rows, :]
    for source in range(1, pool_ref.shape[0] // rows):
        total = total + pool_ref[source * rows : (source + 1) * rows, :]
    return jnp.where(last, total * (LOSS_SCALE / voxels), 1.0)


def out_grad_tile(scale, crop, part, base):
    return base.astype(F32) * scale[crop * 4 + part : crop * 4 + part + 1, :]


def block_kernel(
    where_ref,
    pool_ref,
    base_ref,
    mid1_hbm,
    mid2_hbm,
    turned1_hbm,
    turned2_ref,
    turned_in_hbm,
    spatial_ref,
    expand_ref,
    gain1_ref,
    gain2_ref,
    gain3_ref,
    kept_ref,
    given_ref,
    e_one_ref,
    e_three,
    shifts,
    spatial_sum,
    expand_sum,
    reduce_sum,
    chunk,
    mid1_ref,
    mid2_ref,
    turned1_ref,
    turned_in_ref,
    read_sems,
):
    reads = [
        pltpu.make_async_copy(mid2_hbm, mid2_ref, read_sems.at[0]),
        pltpu.make_async_copy(mid1_hbm, mid1_ref, read_sems.at[1]),
        pltpu.make_async_copy(turned_in_hbm, turned_in_ref, read_sems.at[2]),
        pltpu.make_async_copy(turned1_hbm, turned1_ref, read_sems.at[3]),
    ]
    for read in reads:
        read.start()
    side = 8
    rows, narrow = mid1_ref.shape
    wide = e_three.shape[1]
    crop_rows = rows // MICRO
    plane = side * side
    inverse = 1.0 / (MICRO * 64)
    scale = pooled_scale(where_ref[0] != 0, pool_ref, side * plane)

    step = 256
    for start in range(0, rows, step):
        crop = start // crop_rows
        for part in range(wide // LANES):
            lanes = slice(part * LANES, (part + 1) * LANES)
            at = slice(start, start + step)
            out_grad = out_grad_tile(scale, crop, part, base_ref[at, lanes])
            e_three[at, lanes] = (gain3_ref[:, lanes] * out_grad).astype(BF)

    expand_sum[...] = jnp.dot(turned2_ref[...], e_three[...], preferred_element_type=F32) * inverse
    reads[0].wait()

    for start in range(0, rows, crop_rows):
        at = slice(start, start + crop_rows)
        back = lax.dot_general(
            e_three[at, :], expand_ref[...], ROWS_BY_ROWS, preferred_element_type=F32
        )
        e_two = jnp.where(mid2_ref[at, :].astype(F32) > 0, gain2_ref[...] * back, 0.0)
        e_two = e_two.astype(BF).astype(F32).reshape(plane, side, narrow)
        place = lax.broadcasted_iota(jnp.int32, e_two.shape, 1)
        none = jnp.zeros((side, 1, side, narrow), F32)
        for off_c in (-1, 0, 1):
            if off_c == 0:
                moved = e_two
            elif off_c == 1:
                moved = jnp.where(place == 0, 0.0, pltpu.roll(e_two, 1, 1))
            else:
                moved = jnp.where(place == side - 1, 0.0, pltpu.roll(e_two, side - 1, 1))
            moved = moved.reshape(side, side, side, narrow)
            for off_b in (-1, 0, 1):
                if off_b == 0:
                    both = moved
                elif off_b == 1:
                    both = jnp.concatenate([none, moved[:, :-1]], axis=1)
                else:
                    both = jnp.concatenate([moved[:, 1:], none], axis=1)
                position = 3 * (off_b + 1) + (off_c + 1)
                shifts[at, position * narrow : (position + 1) * narrow] = both.reshape(
                    crop_rows, narrow
                ).astype(BF)

    reads[1].wait()
    empty = jnp.zeros((plane, narrow), F32)
    for crop in range(MICRO):
        at = slice(crop * crop_rows, (crop + 1) * crop_rows)
        spread = lax.dot_general(
            shifts[at, :], spatial_ref[...], ROWS_BY_ROWS, preferred_element_type=F32
        )
        lower = jnp.concatenate([spread[plane:, :narrow], empty], axis=0)
        upper = jnp.concatenate([empty, spread[:-plane, 2 * narrow :]], axis=0)
        back_one = lower + spread[:, narrow : 2 * narrow] + upper
        e_one_ref[at, :] = jnp.where(
            mid1_ref[at, :].astype(F32) > 0, gain1_ref[...] * back_one, 0.0
        ).astype(BF)

    reads[2].wait()
    reduce_sum[...] = (
        jnp.dot(turned_in_ref[...], e_one_ref[...], preferred_element_type=F32) * inverse
    )

    reads[3].wait()
    for off_a in range(3):
        summed = (
            jnp.dot(
                turned1_ref[off_a * narrow : (off_a + 1) * narrow, :],
                shifts[...],
                preferred_element_type=F32,
            )
            * inverse
        )
        for position in range(9):
            block = off_a * 9 + position
            spatial_sum[block * narrow : (block + 1) * narrow, :] = summed[
                :, position * narrow : (position + 1) * narrow
            ]

    chips = 16
    height = kept_ref.shape[0] // chips
    chunk[140:144, :] = jnp.zeros((4, narrow), F32)

    def pack(chip, to, out_ref):
        for half in range(2):
            device = half * 2 * chips + chip * 2 + to
            chunk[half * 8 : half * 8 + 8, :] = reduce_sum[device * 8 : device * 8 + 8, :]
            for part in range(4):
                chunk[16 + half * 8 + part * 2 : 18 + half * 8 + part * 2, :] = expand_sum[
                    device * 2 : device * 2 + 2, part * LANES : (part + 1) * LANES
                ]
            chunk[32 + half * 54 : 86 + half * 54, :] = spatial_sum[
                device * 54 : device * 54 + 54, :
            ]
        out_ref[chip * height : (chip + 1) * height, :] = chunk[...].astype(BF)

    for core in range(2):

        @pl.when(where_ref[1] == core)
        def _(core=core):
            for chip in range(chips):
                pack(chip, core, kept_ref)
                pack(chip, 1 - core, given_ref)


def block_step(place, pool, base, mid1, mid2, turned1, turned2, turned_in, spatial, expand, gains):
    rows, narrow = mid1.shape
    wide = base.shape[1]
    smem = pl.BlockSpec(memory_space=pltpu.SMEM)
    vmem = pl.BlockSpec(memory_space=pltpu.VMEM)
    hbm = pl.BlockSpec(memory_space=pltpu.HBM)
    return pl.pallas_call(
        block_kernel,
        out_shape=(
            jax.ShapeDtypeStruct((16 * 144, narrow), BF),
            jax.ShapeDtypeStruct((16 * 144, narrow), BF),
            jax.ShapeDtypeStruct((rows, narrow), BF),
        ),
        in_specs=[smem, vmem, vmem, hbm, hbm, hbm, vmem, hbm] + [vmem] * 5,
        out_specs=(vmem, vmem, vmem),
        scratch_shapes=[
            pltpu.VMEM((rows, wide), BF),
            pltpu.VMEM((rows, 9 * narrow), BF),
            pltpu.VMEM((27 * narrow, narrow), F32),
            pltpu.VMEM((narrow, wide), F32),
            pltpu.VMEM((wide, narrow), F32),
            pltpu.VMEM((144, narrow), F32),
        ]
        + [pltpu.VMEM(array.shape, BF) for array in (mid1, mid2, turned1, turned_in)]
        + [pltpu.SemaphoreType.DMA((4,))],
        compiler_params=pltpu.CompilerParams(vmem_limit_bytes=VMEM_LIMIT),
        cost_estimate=pl.CostEstimate(
            flops=4_000_000_000, bytes_accessed=6_000_000, transcendentals=0
        ),
        name="block",
    )(
        place,
        pool,
        *in_vmem(base),
        *in_hbm(mid1, mid2, turned1),
        *in_vmem(turned2),
        *in_hbm(turned_in),
        *in_vmem(spatial, expand),
        *gains,
    )


def input_kernel(
    where_ref, pool_ref, base_ref, input_hbm, e_one_ref, reduce_ref, out_ref, input_ref, read_sem
):
    read = pltpu.make_async_copy(input_hbm, input_ref, read_sem.at[0])
    read.start()
    rows, wide = input_ref.shape
    crop_rows = rows // MICRO
    scale = pooled_scale(where_ref[0] != 0, pool_ref, crop_rows)
    read.wait()
    step = 256
    for start in range(0, rows, step):
        at = slice(start, start + step)
        through = lax.dot_general(
            e_one_ref[at, :], reduce_ref[...], ROWS_BY_ROWS, preferred_element_type=F32
        )
        for part in range(wide // LANES):
            lanes = slice(part * LANES, (part + 1) * LANES)
            out_grad = out_grad_tile(scale, start // crop_rows, part, base_ref[at, lanes])
            out_ref[at, lanes] = jnp.where(
                input_ref[at, lanes].astype(F32) > 0, through[:, lanes] + out_grad, 0.0
            ).astype(BF)


def input_step(place, pool, base, input_pre, e_one, reduce):
    smem = pl.BlockSpec(memory_space=pltpu.SMEM)
    vmem = pl.BlockSpec(memory_space=pltpu.VMEM)
    hbm = pl.BlockSpec(memory_space=pltpu.HBM)
    return pl.pallas_call(
        input_kernel,
        out_shape=jax.ShapeDtypeStruct(input_pre.shape, BF),
        in_specs=[smem, vmem, vmem, hbm, vmem, vmem],
        out_specs=vmem,
        scratch_shapes=[pltpu.VMEM(input_pre.shape, BF), pltpu.SemaphoreType.DMA((1,))],
        compiler_params=pltpu.CompilerParams(vmem_limit_bytes=VMEM_LIMIT),
        cost_estimate=pl.CostEstimate(
            flops=200_000_000, bytes_accessed=6_000_000, transcendentals=0
        ),
        name="input_grad",
    )(place, pool, base, *in_hbm(input_pre), e_one, reduce)


def sum_kernel(half_ref, shares_ref, kept_ref, given_ref, total, other):
    height = total.shape[0]
    summed = shares_ref[0:height, :].astype(F32)
    for source in range(1, shares_ref.shape[0] // height):
        summed = summed + shares_ref[source * height : (source + 1) * height, :].astype(F32)
    total[...] = summed
    other[72:80, :] = jnp.zeros((8, LANES), F32)

    def put(target, half):
        target[0:8, :] = total[half * 8 : half * 8 + 8, :]
        target[8:16, :] = total[16 + half * 8 : 24 + half * 8, :]
        target[16:72, :] = total[32 + half * 54 : 88 + half * 54, :]

    @pl.when(half_ref[0] == 0)
    def _():
        put(kept_ref, 0)
        put(other, 1)

    @pl.when(half_ref[0] != 0)
    def _():
        put(kept_ref, 1)
        put(other, 0)

    given_ref[...] = other[...].astype(BF)


def sum_step(half, shares):
    smem = pl.BlockSpec(memory_space=pltpu.SMEM)
    vmem = pl.BlockSpec(memory_space=pltpu.VMEM)
    return pl.pallas_call(
        sum_kernel,
        out_shape=(
            jax.ShapeDtypeStruct((72, LANES), F32),
            jax.ShapeDtypeStruct((80, LANES), BF),
        ),
        in_specs=[smem, vmem],
        out_specs=(vmem, vmem),
        scratch_shapes=[pltpu.VMEM((144, LANES), F32), pltpu.VMEM((80, LANES), F32)],
        compiler_params=pltpu.CompilerParams(vmem_limit_bytes=VMEM_LIMIT),
        name="shares",
    )(half, shares)


def last_kernel(kept_ref, got_ref, reduce_ref, spatial_ref, expand_ref):
    total = kept_ref[...] + got_ref[...].astype(F32)[0:72]
    reduce_ref[...] = total[0:8, :].astype(BF)
    spatial_ref[...] = total[16:70, :].astype(BF)
    expand_ref[...] = jnp.concatenate(
        [total[8 + 2 * part : 10 + 2 * part, :] for part in range(4)], axis=1
    ).astype(BF)


def last_step(kept, got):
    vmem = pl.BlockSpec(memory_space=pltpu.VMEM)
    return pl.pallas_call(
        last_kernel,
        out_shape=(
            jax.ShapeDtypeStruct((8, LANES), BF),
            jax.ShapeDtypeStruct((54, LANES), BF),
            jax.ShapeDtypeStruct((2, 4 * LANES), BF),
        ),
        in_specs=[vmem] * 2,
        out_specs=(vmem,) * 3,
        compiler_params=pltpu.CompilerParams(vmem_limit_bytes=2 * 1024 * 1024),
        name="weight_grads",
    )(kept, got)


def copies(shard, count):
    rows, width = shard.shape
    return jnp.broadcast_to(shard[None], (count, rows, width)).reshape(count * rows, width)


def in_vmem(*arrays):
    return [pltpu.with_memory_space_constraint(array, pltpu.VMEM) for array in arrays]


def in_hbm(*arrays):
    return [pltpu.with_memory_space_constraint(array, pltpu.HBM) for array in arrays]


def shards(
    projections,
    partner,
    plan,
    head_pre,
    head_in,
    head_out,
    final_pre,
    incoming,
    input_pre,
    mid_pre1,
    mid_pre2,
    w_reduce,
    w_spatial,
    w_expand,
    gain1,
    gain2,
    gain3,
):
    row_count = projections.shape[0]
    sections = lax.axis_size("section")
    peers = lax.axis_size(PLANE)
    upper = lax.axis_index("z_hi")
    me = lax.axis_index(PLANE)
    swap_near = [
        (half * sections + s, (1 - half) * sections + (s + sections // 2) % sections)
        for half in range(2)
        for s in range(sections)
    ]
    swap_far = [(0, 1), (1, 0)]
    narrow = w_reduce.shape[2]
    wide = w_expand.shape[2]
    core = lax.axis_index("core")
    section = lax.axis_index("section")
    chips = peers // 2
    other_rows = lax.ppermute(projections, ("z_hi", "section"), swap_near)
    n_reduce, n_spatial = w_reduce.shape[1], w_spatial.shape[1]
    n_expand = w_expand.shape[1] * wide // narrow
    packed = jnp.concatenate(
        [
            w_reduce[0],
            w_expand[0].reshape(n_expand, narrow),
            w_spatial[0],
            w_reduce[0, : 72 - n_reduce - n_expand - n_spatial],
        ],
        axis=0,
    )
    flat_one = mid_pre1.reshape(-1, narrow)
    flat_two = mid_pre2.reshape(-1, narrow)
    flat_in = input_pre.reshape(-1, wide)
    is_last = section == sections - 1
    place = jnp.stack([is_last.astype(jnp.int32), core.astype(jnp.int32)])
    sent, packed = lax.optimization_barrier(
        (copies(jnp.concatenate([projections, other_rows], axis=0), chips), packed)
    )
    near = lax.all_to_all(sent, ("x", "y"), 0, 0, tiled=True)
    far = lax.ppermute(packed, "z_hi", swap_far)
    ordered = jnp.where(
        upper == 0,
        jnp.concatenate([packed, far], axis=0),
        jnp.concatenate([far, packed], axis=0),
    )
    near, weights = lax.optimization_barrier((near, copies(ordered, chips)))
    across = lax.ppermute(near, "core", swap_far)
    half_crops = peers * row_count
    partner_device = partner % half_crops // row_count
    partner_row = (
        jnp.where(partner_device % 2 == core, 0, half_crops)
        + partner_device // 2 * (2 * row_count)
        + jnp.where(partner // half_crops == upper, 0, row_count)
        + partner % row_count
    )

    weights_near = lax.all_to_all(weights, ("x", "y"), 0, 0, tiled=True)
    projection_gradient, pool_copies = loss_step(
        (me // 2 * 2 * row_count).reshape(1),
        plan,
        near,
        across,
        partner_row.reshape(-1, 1),
        head_pre,
        head_in,
        head_out,
        row_count,
        sections,
    )
    pool = lax.all_to_all(pool_copies, "section", 0, 0, tiled=True)
    weights_near, pool_copies = lax.optimization_barrier((weights_near, pool_copies))
    weights_across = lax.ppermute(weights_near, "core", swap_far)
    place, weights_across = lax.optimization_barrier((place, weights_across))
    turned_one, turned_two, turned_in, base = prepare_step(
        place,
        final_pre.reshape(-1, wide),
        incoming.reshape(-1, wide),
        flat_one,
        flat_two,
        flat_in,
    )
    full_spatial, full_expand, full_reduce = unpack_step(
        place, weights_near, weights_across, wide
    )
    kept, given, e_one = block_step(
        place,
        pool,
        base,
        flat_one,
        flat_two,
        turned_one,
        turned_two,
        turned_in,
        full_spatial,
        full_expand,
        (gain1, gain2, gain3),
    )
    got = lax.ppermute(given, "core", swap_far)
    paired = (kept.astype(F32) + got.astype(F32)).astype(BF)
    shares = lax.all_to_all(paired, ("x", "y"), 0, 0, tiled=True)
    input_grad = input_step(place, pool, base, flat_in, e_one, full_reduce)
    kept, given = sum_step(upper.astype(jnp.int32).reshape(1), shares)
    got = lax.ppermute(given, "z_hi", swap_far)
    sum_reduce, sum_spatial, sum_expand = last_step(kept, got)
    return (
        projection_gradient,
        input_grad.reshape(input_pre.shape),
        sum_reduce[None],
        sum_spatial[None],
        sum_expand[None],
    )


def solution(mesh):
    fine = Mesh(
        mesh.devices.reshape(2, 4, 4, 2, mesh.shape["section"]),
        ("z_hi", "x", "y", "core", "section"),
    )
    placed = (
        P(DP, None),
        P(DP),
        P(DP, None),
        P(DP, "section"),
        P(None, "section"),
        P("section", None),
        P(DP, None, None, None, None),
        P("section", DP, None, None, None, None),
        P("section", DP, None, None, None, None),
        P("section", DP, None, None, None, None),
        P("section", DP, None, None, None, None),
        P("section", DP, None),
        P("section", DP, None),
        P("section", DP, None),
        P("section", None),
        P("section", None),
        P("section", None),
    )
    return jax.shard_map(
        shards,
        mesh=fine,
        in_specs=placed,
        out_specs=(
            P(DP, None),
            P("section", DP, None, None, None, None),
            P("section", DP, None),
            P("section", DP, None),
            P("section", DP, None),
        ),
        check_vma=False,
    )
```

profile of v0, /device:TPU:2, one launch (start us, length us, event | category | flops | bytes accessed | tf_op | source)
XLA Modules:
  0.0 126.5 jit_solution(5629517614385109347)
XLA Ops:
  0.6 12.7 %collective-permute-start = (f32[32,128]{1,0:T(8,128)}, f32[32,128]{1,0:T(8,128)S(1)}, u32[]{:S(2)}, u32[]{:S(2)}) collective-permute-start(f32[32,128]{1,0:T(8,128)} %param.17), channel_id=1, source_target_pairs={{0,260},{1,261},{2,262},{3,263},{4,256},{5,257},{6,258},{7,259},{2... | collective-permute-start | bytes 49160 | tf_op jit(solution)/shard_map/ppermute | solution.py:697
  13.4 0.7 slice_bitcast_fusion
  14.1 0.7 reshape_squeeze.3
  14.8 0.7 pad_maximum_fusion.1
  15.5 0.0 collective-permute-done
  15.5 0.7 pad_maximum_fusion
  16.2 0.8 broadcast_in_dim.27
  17.1 7.5 %all-to-all-start = ((f32[16,64,128]{2,1,0:T(8,128)}), f32[16,64,128]{2,1,0:T(8,128)S(1)}, u32[]{:S(2)}, u32[]{:S(2)}) async-start(f32[16,64,128]{2,1,0:T(8,128)} %bitcast.5), calls=%async_computation | async-start | bytes 1048576 | tf_op jit(solution)/shard_map/all_to_all | solution.py:717
  24.5 0.0 copy-start.1
  24.5 0.0 copy-start.3
  24.6 0.0 copy-start.4
  24.6 10.8 %collective-permute-start.1 = (bf16[72,128]{1,0:T(8,128)(2,1)S(1)}, bf16[72,128]{1,0:T(8,128)(2,1)S(1)}, u32[]{:S(2)}, u32[]{:S(2)}) collective-permute-start(bf16[72,128]{1,0:T(8,128)(2,1)S(1)} %pad_maximum_fusion.1), channel_id=1, source_target_pairs={{0,256},{256,0},{1,257},{257,1},{2,258},{258,2},{3,259},{259,3},{4... | collective-permute-start | bytes 55304 | tf_op jit(solution)/shard_map/ppermute | solution.py:718
  35.3 3.7 %collective-permute-done.1 = bf16[72,128]{1,0:T(8,128)(2,1)S(1)} collective-permute-done((bf16[72,128]{1,0:T(8,128)(2,1)S(1)}, bf16[72,128]{1,0:T(8,128)(2,1)S(1)}, u32[]{:S(2)}, u32[]{:S(2)}) %collective-permute-start.1) | collective-permute-done | bytes 18464 | tf_op jit(solution)/shard_map/ppermute | solution.py:718
  39.1 0.0 all-to-all-done
  39.1 0.9 broadcast_in_dim.28
  40.0 1.9 %collective-permute-start.2 = (f32[1024,128]{1,0:T(8,128)S(1)}, f32[1024,128]{1,0:T(8,128)S(1)}, u32[]{:S(2)}, u32[]{:S(2)}) collective-permute-start(f32[1024,128]{1,0:T(8,128)S(1)} %bitcast.32), channel_id=1, source_target_pairs={{0,8},{8,0},{1,9},{9,1},{2,10},{10,2},{3,11},{11,3},{4,12},{12,4},... | collective-permute-start | bytes 1572872 | tf_op jit(solution)/shard_map/ppermute | solution.py:725
  41.9 0.0 copy-done.7
  42.0 0.1 copy.22.partner_ref
  42.1 7.2 %all-to-all-start.1 = ((bf16[16,144,128]{2,1,0:T(8,128)(2,1)}), bf16[16,144,128]{2,1,0:T(8,128)(2,1)S(1)}, u32[]{:S(2)}, u32[]{:S(2)}) async-start(bf16[16,144,128]{2,1,0:T(8,128)(2,1)} %bitcast.11), calls=%async_computation.1 | async-start | bytes 1179648 | tf_op jit(solution)/shard_map/all_to_all | solution.py:735
  49.3 0.0 collective-permute-done.2.across_ref
  49.3 0.0 copy-done
  49.3 0.0 copy-done.1
  49.3 0.0 copy-done.3
  49.3 0.0 copy-done.4
  49.3 13.8 %loss.1 = (f32[32,128]{1,0:T(8,128)}, f32[64,128]{1,0:T(8,128)}) custom-call(s32[1]{0:T(128)} %bitcast.where_ref, s32[1,32]{1,0:T(1,128)S(1)} %copy-done.4, f32[1024,128]{1,0:T(8,128)S(1)} %bitcast.33, f32[1024,128]{1,0:T(8,128)S(1)} %collective-permute-done.2.across_ref, s32[32,1]{1,0:T(8,128)S(1)} %copy.22.partner_ref, bf16[2,256]{1,0:T(2,128)(2,1)S(1)} %copy-done.3, ...), custom_call_target="tpu_custom_call" | custom-call | flops 12000000000 | bytes 2000000 | tf_op jit(solution)/shard_map/loss/pallas_call | solution.py:316
  63.1 0.0 all-to-all-done.1
  63.1 1.9 %collective-permute-start.3 = (bf16[2304,128]{1,0:T(8,128)(2,1)S(1)}, bf16[2304,128]{1,0:T(8,128)(2,1)S(1)}, u32[]{:S(2)}, u32[]{:S(2)}) collective-permute-start(bf16[2304,128]{1,0:T(8,128)(2,1)S(1)} %bitcast.29), channel_id=1, source_target_pairs={{0,8},{8,0},{1,9},{9,1},{2,10},{10,2},{3,11},{11,3},{4,12},{12,4},... | collective-permute-start | bytes 1769480 | tf_op jit(solution)/shard_map/ppermute | solution.py:750
  65.0 7.5 %all-to-all-start.2 = ((f32[8,8,128]{2,1,0:T(8,128)}), f32[8,8,128]{2,1,0:T(8,128)S(1)}, u32[]{:S(2)}, u32[]{:S(2)}) async-start(f32[8,8,128]{2,1,0:T(8,128)} %bitcast.13), calls=%async_computation.2 | async-start | bytes 65536 | tf_op jit(solution)/shard_map/all_to_all | solution.py:748
  72.5 0.1 pad_add_fusion.where_ref
  72.6 0.0 collective-permute-done.3.across_ref
  72.6 1.0 unpack.1
  73.5 0.0 copy-start.2
  73.5 0.0 copy-start.5
  73.6 0.0 copy-start.6
  73.6 3.9 %prepare.1 = (bf16[384,1024]{1,0:T(8,128)(2,1)}, bf16[128,1024]{1,0:T(8,128)(2,1)S(1)}, bf16[512,1024]{1,0:T(8,128)(2,1)}, bf16[1024,512]{1,0:T(8,128)(2,1)S(1)}) custom-call(s32[2]{0:T(128)S(1)} %pad_add_fusion.where_ref, bf16[1024,512]{1,0:T(8,128)(2,1)} %bitcast.39, bf16[1024,512]{1,0:T(8,128)(2,1)} %bitcast.40, bf16[1024,128]{1,0:T(8,128)(2,1)} %bitcast.42, ...), custom_call_target="tpu_custom_call" | custom-call | bytes 6000000 | tf_op jit(solution)/shard_map/prepare/pallas_call | solution.py:110
  77.5 5.6 %all-to-all-done.2 = f32[8,8,128]{2,1,0:T(8,128)S(1)} async-done(((f32[8,8,128]{2,1,0:T(8,128)}), f32[8,8,128]{2,1,0:T(8,128)S(1)}, u32[]{:S(2)}, u32[]{:S(2)}) %all-to-all-start.2) | async-done | bytes 32800 | tf_op jit(solution)/shard_map/all_to_all | solution.py:748
  83.1 0.0 copy-done.2
  83.1 0.0 copy-done.5
  83.1 6.1 %block.1 = (bf16[2304,128]{1,0:T(8,128)(2,1)S(1)}, bf16[2304,128]{1,0:T(8,128)(2,1)S(1)}, bf16[1024,128]{1,0:T(8,128)(2,1)S(1)}) custom-call(s32[2]{0:T(128)S(1)} %pad_add_fusion.where_ref, f32[64,128]{1,0:T(8,128)S(1)} %bitcast.34, bf16[1024,512]{1,0:T(8,128)(2,1)S(1)} %get-tuple-element.37.base_ref, bf16[1024,128]{1,0:T(8,128)(2,1)} %bitcast.43, ...), custom_call_target="tpu_custom_call" | custom-call | flops 4000000000 | bytes 6000000 | tf_op jit(solution)/shard_map/block/pallas_call | solution.py:504
  89.2 1.9 %collective-permute-start.4 = (bf16[2304,128]{1,0:T(8,128)(2,1)S(1)}, bf16[2304,128]{1,0:T(8,128)(2,1)S(1)}, u32[]{:S(2)}, u32[]{:S(2)}) collective-permute-start(bf16[2304,128]{1,0:T(8,128)(2,1)S(1)} %get-tuple-element.47), channel_id=1, source_target_pairs={{0,8},{8,0},{1,9},{9,1},{2,10},{10,2},{3,11},{11,3},{4,12},{12,4},... | collective-permute-start | bytes 1769480 | tf_op jit(solution)/shard_map/ppermute | solution.py:776
  91.1 2.0 %collective-permute-done.4 = bf16[2304,128]{1,0:T(8,128)(2,1)S(1)} collective-permute-done((bf16[2304,128]{1,0:T(8,128)(2,1)S(1)}, bf16[2304,128]{1,0:T(8,128)(2,1)S(1)}, u32[]{:S(2)}, u32[]{:S(2)}) %collective-permute-start.4) | collective-permute-done | bytes 589856 | tf_op jit(solution)/shard_map/ppermute | solution.py:776
  93.1 0.2 add_convert_fusion
  93.2 18.1 %all_to_all.46 = bf16[16,144,128]{2,1,0:T(8,128)(2,1)S(1)} all-to-all(bf16[16,144,128]{2,1,0:T(8,128)(2,1)S(1)} %bitcast.38), channel_id=1, replica_groups=mesh['z_hi'=2,'x'=4,'y'=4,'core'=2,'section'=8] {'x','y'}, dimensions={0} | all-to-all | bytes 1179648 | tf_op jit(solution)/shard_map/all_to_all | solution.py:778
  111.4 0.1 shares.1
  111.5 8.2 %collective-permute-start.5 = (bf16[80,128]{1,0:T(8,128)(2,1)S(1)}, bf16[80,128]{1,0:T(8,128)(2,1)S(1)}, u32[]{:S(2)}, u32[]{:S(2)}) collective-permute-start(bf16[80,128]{1,0:T(8,128)(2,1)S(1)} %get-tuple-element.49), channel_id=1, source_target_pairs={{0,256},{256,0},{1,257},{257,1},{2,258},{258,2},{3,259},{259,3},{4... | collective-permute-start | bytes 61448 | tf_op jit(solution)/shard_map/ppermute | solution.py:781
  119.7 3.4 %input_grad.1 = bf16[1024,512]{1,0:T(8,128)(2,1)} custom-call(s32[2]{0:T(128)S(1)} %pad_add_fusion.where_ref, f32[64,128]{1,0:T(8,128)S(1)} %bitcast.35, bf16[1024,512]{1,0:T(8,128)(2,1)S(1)} %get-tuple-element.37.base_ref, bf16[1024,512]{1,0:T(8,128)(2,1)} %bitcast.37, bf16[1024,128]{1,0:T(8,128)(2,1)S(1)} %get-tuple-element.44.e_one_ref, ...), custom_call_target="tpu_custom_call" | custom-call | flops 200000000 | bytes 6000000 | tf_op jit(solution)/shard_map/input_grad/pallas_call | solution.py:567
  123.1 2.8 %collective-permute-done.5.got_ref = bf16[80,128]{1,0:T(8,128)(2,1)S(1)} collective-permute-done((bf16[80,128]{1,0:T(8,128)(2,1)S(1)}, bf16[80,128]{1,0:T(8,128)(2,1)S(1)}, u32[]{:S(2)}, u32[]{:S(2)}) %collective-permute-start.5) | collective-permute-done | bytes 20512 | tf_op jit(solution)/shard_map/ppermute | solution.py:781
  125.9 0.6 weight_grads.1
  (5 shorter events, 0.0 us)
Async XLA Ops:
  0.6 14.8 %collective-permute-start = (f32[32,128]{1,0:T(8,128)}, f32[32,128]{1,0:T(8,128)S(1)}, u32[]{:S(2)}, u32[]{:S(2)}) collective-permute-start(f32[32,128]{1,0:T(8,128)} %param.17), channel_id=1, source_target_pairs={{0,260},{1,261},{2,262},{3,263},{4,256},{5,257},{6,258},{7,259},{2... | collective-permute-start | bytes 49160 | tf_op jit(solution)/shard_map/ppermute | solution.py:697
  16.2 25.7 %copy-start.7 = (s32[32]{0:T(128)S(1)}, s32[32]{0:T(128)}, u32[]{:S(2)}) copy-start(s32[32]{0:T(128)} %param.18) | copy-start | bytes 388
  17.1 22.0 %all-to-all-start = ((f32[16,64,128]{2,1,0:T(8,128)}), f32[16,64,128]{2,1,0:T(8,128)S(1)}, u32[]{:S(2)}, u32[]{:S(2)}) async-start(f32[16,64,128]{2,1,0:T(8,128)} %bitcast.5), calls=%async_computation | async-start | bytes 1048576 | tf_op jit(solution)/shard_map/all_to_all | solution.py:717
  24.5 24.8 %copy-start = (bf16[512,256]{1,0:T(8,128)(2,1)S(1)}, bf16[512,256]{1,0:T(8,128)(2,1)}, u32[]{:S(2)}) copy-start(bf16[512,256]{1,0:T(8,128)(2,1)} %head_in_ref.1) | copy-start | bytes 786436
  24.5 24.8 %copy-start.1 = (bf16[256,128]{1,0:T(8,128)(2,1)S(1)}, bf16[256,128]{1,0:T(8,128)(2,1)}, u32[]{:S(2)}) copy-start(bf16[256,128]{1,0:T(8,128)(2,1)} %head_out_ref.1) | copy-start | bytes 196612
  24.5 24.8 %copy-start.3 = (bf16[2,256]{1,0:T(2,128)(2,1)S(1)}, bf16[2,256]{1,0:T(2,128)(2,1)}, u32[]{:S(2)}) copy-start(bf16[2,256]{1,0:T(2,128)(2,1)} %head_pre_ref.1) | copy-start | bytes 3076
  24.6 24.8 %copy-start.4 = (s32[1,32]{1,0:T(1,128)S(1)}, s32[1,32]{1,0:T(1,128)}, u32[]{:S(2)}) copy-start(s32[1,32]{1,0:T(1,128)} %plan_ref.1) | copy-start | bytes 388
  24.6 14.5 %collective-permute-start.1 = (bf16[72,128]{1,0:T(8,128)(2,1)S(1)}, bf16[72,128]{1,0:T(8,128)(2,1)S(1)}, u32[]{:S(2)}, u32[]{:S(2)}) collective-permute-start(bf16[72,128]{1,0:T(8,128)(2,1)S(1)} %pad_maximum_fusion.1), channel_id=1, source_target_pairs={{0,256},{256,0},{1,257},{257,1},{2,258},{258,2},{3,259},{259,3},{4... | collective-permute-start | bytes 55304 | tf_op jit(solution)/shard_map/ppermute | solution.py:718
  40.0 9.3 %collective-permute-start.2 = (f32[1024,128]{1,0:T(8,128)S(1)}, f32[1024,128]{1,0:T(8,128)S(1)}, u32[]{:S(2)}, u32[]{:S(2)}) collective-permute-start(f32[1024,128]{1,0:T(8,128)S(1)} %bitcast.32), channel_id=1, source_target_pairs={{0,8},{8,0},{1,9},{9,1},{2,10},{10,2},{3,11},{11,3},{4,12},{12,4},... | collective-permute-start | bytes 1572872 | tf_op jit(solution)/shard_map/ppermute | solution.py:725
  42.1 21.1 %all-to-all-start.1 = ((bf16[16,144,128]{2,1,0:T(8,128)(2,1)}), bf16[16,144,128]{2,1,0:T(8,128)(2,1)S(1)}, u32[]{:S(2)}, u32[]{:S(2)}) async-start(bf16[16,144,128]{2,1,0:T(8,128)(2,1)} %bitcast.11), calls=%async_computation.1 | async-start | bytes 1179648 | tf_op jit(solution)/shard_map/all_to_all | solution.py:735
  63.1 9.4 %collective-permute-start.3 = (bf16[2304,128]{1,0:T(8,128)(2,1)S(1)}, bf16[2304,128]{1,0:T(8,128)(2,1)S(1)}, u32[]{:S(2)}, u32[]{:S(2)}) collective-permute-start(bf16[2304,128]{1,0:T(8,128)(2,1)S(1)} %bitcast.29), channel_id=1, source_target_pairs={{0,8},{8,0},{1,9},{9,1},{2,10},{10,2},{3,11},{11,3},{4,12},{12,4},... | collective-permute-start | bytes 1769480 | tf_op jit(solution)/shard_map/ppermute | solution.py:750
  65.0 18.1 %all-to-all-start.2 = ((f32[8,8,128]{2,1,0:T(8,128)}), f32[8,8,128]{2,1,0:T(8,128)S(1)}, u32[]{:S(2)}, u32[]{:S(2)}) async-start(f32[8,8,128]{2,1,0:T(8,128)} %bitcast.13), calls=%async_computation.2 | async-start | bytes 65536 | tf_op jit(solution)/shard_map/all_to_all | solution.py:748
  73.5 9.6 %copy-start.2 = (f32[1,512]{1,0:T(1,128)S(1)}, f32[1,512]{1,0:T(1,128)}, u32[]{:S(2)}) copy-start(f32[1,512]{1,0:T(1,128)} %gain3_ref.1) | copy-start | bytes 6148
  73.5 9.6 %copy-start.5 = (f32[1,128]{1,0:T(1,128)S(1)}, f32[1,128]{1,0:T(1,128)}, u32[]{:S(2)}) copy-start(f32[1,128]{1,0:T(1,128)} %gain1_ref.1) | copy-start | bytes 1540
  73.6 9.6 %copy-start.6 = (f32[1,128]{1,0:T(1,128)S(1)}, f32[1,128]{1,0:T(1,128)}, u32[]{:S(2)}) copy-start(f32[1,128]{1,0:T(1,128)} %gain2_ref.1) | copy-start | bytes 1540
  89.2 3.9 %collective-permute-start.4 = (bf16[2304,128]{1,0:T(8,128)(2,1)S(1)}, bf16[2304,128]{1,0:T(8,128)(2,1)S(1)}, u32[]{:S(2)}, u32[]{:S(2)}) collective-permute-start(bf16[2304,128]{1,0:T(8,128)(2,1)S(1)} %get-tuple-element.47), channel_id=1, source_target_pairs={{0,8},{8,0},{1,9},{9,1},{2,10},{10,2},{3,11},{11,3},{4,12},{12,4},... | collective-permute-start | bytes 1769480 | tf_op jit(solution)/shard_map/ppermute | solution.py:776
  111.5 14.4 %collective-permute-start.5 = (bf16[80,128]{1,0:T(8,128)(2,1)S(1)}, bf16[80,128]{1,0:T(8,128)(2,1)S(1)}, u32[]{:S(2)}, u32[]{:S(2)}) collective-permute-start(bf16[80,128]{1,0:T(8,128)(2,1)S(1)} %get-tuple-element.49), channel_id=1, source_target_pairs={{0,256},{256,0},{1,257},{257,1},{2,258},{258,2},{3,259},{259,3},{4... | collective-permute-start | bytes 61448 | tf_op jit(solution)/shard_map/ppermute | solution.py:781
where the time goes:
time: 127 us; the launch traced here: 126 us
  starting transfers between devices  59.6 us (47%)
  Pallas kernels  28.8 us (23%)
  blocking collectives  18.1 us (14%)
  waiting for transfers between devices  14.1 us (11%)
  local copies, waits for them, and re-layouts  3.25 us (3%)
  other arithmetic  1.72 us (1%)
    all_to_all x1, blocking collectives, shards(): shares = lax.all_to_all(paired, ('x', 'y'), 0, 0, tiled=True)  18.1 us
    pallas_call x1, Pallas kernels, loss_step(): pl.pallas_call(loss_kernel, out_shape=(jax.ShapeDtypeStruct((own, width),...  13.8 us
    ppermute x1, starting transfers between devices, shards(): other_rows = lax.ppermute(projections, ('z_hi', 'section'), swap_near)  12.7 us
    ppermute x1, starting transfers between devices, shards(): far = lax.ppermute(packed, 'z_hi', swap_far)  10.8 us
    ppermute x1, starting transfers between devices, shards(): got = lax.ppermute(given, 'z_hi', swap_far)  8.24 us
    all_to_all x1, starting transfers between devices, shards(): near = lax.all_to_all(sent, ('x', 'y'), 0, 0, tiled=True)  7.48 us
    all_to_all x1, starting transfers between devices, shards(): pool = lax.all_to_all(pool_copies, 'section', 0, 0, tiled=True)  7.45 us
    all_to_all x1, starting transfers between devices, shards(): weights_near = lax.all_to_all(weights, ('x', 'y'), 0, 0, tiled=True)  7.23 us
  transfers between devices with their start and end apart: 9, of which 4 were waited for; matrix products, arithmetic and copies ran while one was open for 2% of the time, Pallas kernels for 17%

commit v1 on v0

--- a/solution.py
+++ b/solution.py
@@ -380,8 +380,8 @@
     reads = [
         pltpu.make_async_copy(mid2_hbm, mid2_ref, read_sems.at[0]),
         pltpu.make_async_copy(mid1_hbm, mid1_ref, read_sems.at[1]),
-        pltpu.make_async_copy(turned_in_hbm, turned_in_ref, read_sems.at[2]),
-        pltpu.make_async_copy(turned1_hbm, turned1_ref, read_sems.at[3]),
+        pltpu.make_async_copy(turned1_hbm, turned1_ref, read_sems.at[2]),
+        pltpu.make_async_copy(turned_in_hbm, turned_in_ref, read_sems.at[3]),
     ]
     for read in reads:
         read.start()
@@ -449,11 +449,6 @@
         ).astype(BF)
 
     reads[2].wait()
-    reduce_sum[...] = (
-        jnp.dot(turned_in_ref[...], e_one_ref[...], preferred_element_type=F32) * inverse
-    )
-
-    reads[3].wait()
     for off_a in range(3):
         summed = (
             jnp.dot(
@@ -468,6 +463,11 @@
             spatial_sum[block * narrow : (block + 1) * narrow, :] = summed[
                 :, position * narrow : (position + 1) * narrow
             ]
+
+    reads[3].wait()
+    reduce_sum[...] = (
+        jnp.dot(turned_in_ref[...], e_one_ref[...], preferred_element_type=F32) * inverse
+    )
 
     chips = 16
     height = kept_ref.shape[0] // chips

time: 127 us -> 127 us (level)
  no operation moved by 1% of the time
where the time goes in v1:
time: 127 us; the launch traced here: 126 us
  starting transfers between devices  59.6 us (47%)
  Pallas kernels  28.7 us (23%)
  blocking collectives  18.1 us (14%)
  waiting for transfers between devices  14.1 us (11%)
  local copies, waits for them, and re-layouts  3.25 us (3%)
  other arithmetic  1.72 us (1%)
    all_to_all x1, blocking collectives, shards(): shares = lax.all_to_all(paired, ('x', 'y'), 0, 0, tiled=True)  18.1 us
    pallas_call x1, Pallas kernels, loss_step(): pl.pallas_call(loss_kernel, out_shape=(jax.ShapeDtypeStruct((own, width),...  13.8 us
    ppermute x1, starting transfers between devices, shards(): other_rows = lax.ppermute(projections, ('z_hi', 'section'), swap_near)  12.7 us
    ppermute x1, starting transfers between devices, shards(): far = lax.ppermute(packed, 'z_hi', swap_far)  10.8 us
    ppermute x1, starting transfers between devices, shards(): got = lax.ppermute(given, 'z_hi', swap_far)  8.24 us
    all_to_all x1, starting transfers between devices, shards(): near = lax.all_to_all(sent, ('x', 'y'), 0, 0, tiled=True)  7.48 us
    all_to_all x1, starting transfers between devices, shards(): pool = lax.all_to_all(pool_copies, 'section', 0, 0, tiled=True)  7.45 us
    all_to_all x1, starting transfers between devices, shards(): weights_near = lax.all_to_all(weights, ('x', 'y'), 0, 0, tiled=True)  7.23 us
  transfers between devices with their start and end apart: 9, of which 4 were waited for; matrix products, arithmetic and copies ran while one was open for 2% of the time, Pallas kernels for 17%

profile of v1, /device:TPU:2, one launch (start us, length us, event | category | flops | bytes accessed | tf_op | source)
XLA Modules:
  0.0 126.4 jit_solution(2856470376329914218)
XLA Ops:
  0.6 12.7 %collective-permute-start = (f32[32,128]{1,0:T(8,128)}, f32[32,128]{1,0:T(8,128)S(1)}, u32[]{:S(2)}, u32[]{:S(2)}) collective-permute-start(f32[32,128]{1,0:T(8,128)} %param.17), channel_id=1, source_target_pairs={{0,260},{1,261},{2,262},{3,263},{4,256},{5,257},{6,258},{7,259},{2... | collective-permute-start | bytes 49160 | tf_op jit(solution)/shard_map/ppermute | solution.py:697
  13.4 0.7 slice_bitcast_fusion
  14.1 0.7 reshape_squeeze.3
  14.8 0.7 pad_maximum_fusion.1
  15.5 0.0 collective-permute-done
  15.5 0.7 pad_maximum_fusion
  16.2 0.8 broadcast_in_dim.27
  17.1 7.5 %all-to-all-start = ((f32[16,64,128]{2,1,0:T(8,128)}), f32[16,64,128]{2,1,0:T(8,128)S(1)}, u32[]{:S(2)}, u32[]{:S(2)}) async-start(f32[16,64,128]{2,1,0:T(8,128)} %bitcast.5), calls=%async_computation | async-start | bytes 1048576 | tf_op jit(solution)/shard_map/all_to_all | solution.py:717
  24.5 0.0 copy-start.1
  24.5 0.0 copy-start.3
  24.6 0.0 copy-start.4
  24.6 10.8 %collective-permute-start.1 = (bf16[72,128]{1,0:T(8,128)(2,1)S(1)}, bf16[72,128]{1,0:T(8,128)(2,1)S(1)}, u32[]{:S(2)}, u32[]{:S(2)}) collective-permute-start(bf16[72,128]{1,0:T(8,128)(2,1)S(1)} %pad_maximum_fusion.1), channel_id=1, source_target_pairs={{0,256},{256,0},{1,257},{257,1},{2,258},{258,2},{3,259},{259,3},{4... | collective-permute-start | bytes 55304 | tf_op jit(solution)/shard_map/ppermute | solution.py:718
  35.3 3.7 %collective-permute-done.1 = bf16[72,128]{1,0:T(8,128)(2,1)S(1)} collective-permute-done((bf16[72,128]{1,0:T(8,128)(2,1)S(1)}, bf16[72,128]{1,0:T(8,128)(2,1)S(1)}, u32[]{:S(2)}, u32[]{:S(2)}) %collective-permute-start.1) | collective-permute-done | bytes 18464 | tf_op jit(solution)/shard_map/ppermute | solution.py:718
  39.1 0.0 all-to-all-done
  39.1 0.9 broadcast_in_dim.28
  40.0 1.9 %collective-permute-start.2 = (f32[1024,128]{1,0:T(8,128)S(1)}, f32[1024,128]{1,0:T(8,128)S(1)}, u32[]{:S(2)}, u32[]{:S(2)}) collective-permute-start(f32[1024,128]{1,0:T(8,128)S(1)} %bitcast.32), channel_id=1, source_target_pairs={{0,8},{8,0},{1,9},{9,1},{2,10},{10,2},{3,11},{11,3},{4,12},{12,4},... | collective-permute-start | bytes 1572872 | tf_op jit(solution)/shard_map/ppermute | solution.py:725
  41.9 0.0 copy-done.7
  42.0 0.1 copy.22.partner_ref
  42.1 7.2 %all-to-all-start.1 = ((bf16[16,144,128]{2,1,0:T(8,128)(2,1)}), bf16[16,144,128]{2,1,0:T(8,128)(2,1)S(1)}, u32[]{:S(2)}, u32[]{:S(2)}) async-start(bf16[16,144,128]{2,1,0:T(8,128)(2,1)} %bitcast.11), calls=%async_computation.1 | async-start | bytes 1179648 | tf_op jit(solution)/shard_map/all_to_all | solution.py:735
  49.3 0.0 collective-permute-done.2.across_ref
  49.3 0.0 copy-done
  49.3 0.0 copy-done.1
  49.3 0.0 copy-done.3
  49.3 0.0 copy-done.4
  49.3 13.8 %loss.1 = (f32[32,128]{1,0:T(8,128)}, f32[64,128]{1,0:T(8,128)}) custom-call(s32[1]{0:T(128)} %bitcast.where_ref, s32[1,32]{1,0:T(1,128)S(1)} %copy-done.4, f32[1024,128]{1,0:T(8,128)S(1)} %bitcast.33, f32[1024,128]{1,0:T(8,128)S(1)} %collective-permute-done.2.across_ref, s32[32,1]{1,0:T(8,128)S(1)} %copy.22.partner_ref, bf16[2,256]{1,0:T(2,128)(2,1)S(1)} %copy-done.3, ...), custom_call_target="tpu_custom_call" | custom-call | flops 12000000000 | bytes 2000000 | tf_op jit(solution)/shard_map/loss/pallas_call | solution.py:316
  63.1 0.0 all-to-all-done.1
  63.1 1.9 %collective-permute-start.3 = (bf16[2304,128]{1,0:T(8,128)(2,1)S(1)}, bf16[2304,128]{1,0:T(8,128)(2,1)S(1)}, u32[]{:S(2)}, u32[]{:S(2)}) collective-permute-start(bf16[2304,128]{1,0:T(8,128)(2,1)S(1)} %bitcast.29), channel_id=1, source_target_pairs={{0,8},{8,0},{1,9},{9,1},{2,10},{10,2},{3,11},{11,3},{4,12},{12,4},... | collective-permute-start | bytes 1769480 | tf_op jit(solution)/shard_map/ppermute | solution.py:750
  65.0 7.5 %all-to-all-start.2 = ((f32[8,8,128]{2,1,0:T(8,128)}), f32[8,8,128]{2,1,0:T(8,128)S(1)}, u32[]{:S(2)}, u32[]{:S(2)}) async-start(f32[8,8,128]{2,1,0:T(8,128)} %bitcast.13), calls=%async_computation.2 | async-start | bytes 65536 | tf_op jit(solution)/shard_map/all_to_all | solution.py:748
  72.5 0.1 pad_add_fusion.where_ref
  72.6 0.0 collective-permute-done.3.across_ref
  72.6 1.0 unpack.1
  73.5 0.0 copy-start.2
  73.5 0.0 copy-start.5
  73.6 0.0 copy-start.6
  73.6 3.9 %prepare.1 = (bf16[384,1024]{1,0:T(8,128)(2,1)}, bf16[128,1024]{1,0:T(8,128)(2,1)S(1)}, bf16[512,1024]{1,0:T(8,128)(2,1)}, bf16[1024,512]{1,0:T(8,128)(2,1)S(1)}) custom-call(s32[2]{0:T(128)S(1)} %pad_add_fusion.where_ref, bf16[1024,512]{1,0:T(8,128)(2,1)} %bitcast.39, bf16[1024,512]{1,0:T(8,128)(2,1)} %bitcast.40, bf16[1024,128]{1,0:T(8,128)(2,1)} %bitcast.42, ...), custom_call_target="tpu_custom_call" | custom-call | bytes 6000000 | tf_op jit(solution)/shard_map/prepare/pallas_call | solution.py:110
  77.5 5.6 %all-to-all-done.2 = f32[8,8,128]{2,1,0:T(8,128)S(1)} async-done(((f32[8,8,128]{2,1,0:T(8,128)}), f32[8,8,128]{2,1,0:T(8,128)S(1)}, u32[]{:S(2)}, u32[]{:S(2)}) %all-to-all-start.2) | async-done | bytes 32800 | tf_op jit(solution)/shard_map/all_to_all | solution.py:748
  83.1 0.0 copy-done.2
  83.1 0.0 copy-done.5
  83.1 6.0 %block.1 = (bf16[2304,128]{1,0:T(8,128)(2,1)S(1)}, bf16[2304,128]{1,0:T(8,128)(2,1)S(1)}, bf16[1024,128]{1,0:T(8,128)(2,1)S(1)}) custom-call(s32[2]{0:T(128)S(1)} %pad_add_fusion.where_ref, f32[64,128]{1,0:T(8,128)S(1)} %bitcast.34, bf16[1024,512]{1,0:T(8,128)(2,1)S(1)} %get-tuple-element.37.base_ref, bf16[1024,128]{1,0:T(8,128)(2,1)} %bitcast.43, ...), custom_call_target="tpu_custom_call" | custom-call | flops 4000000000 | bytes 6000000 | tf_op jit(solution)/shard_map/block/pallas_call | solution.py:504
  89.1 1.9 %collective-permute-start.4 = (bf16[2304,128]{1,0:T(8,128)(2,1)S(1)}, bf16[2304,128]{1,0:T(8,128)(2,1)S(1)}, u32[]{:S(2)}, u32[]{:S(2)}) collective-permute-start(bf16[2304,128]{1,0:T(8,128)(2,1)S(1)} %get-tuple-element.47), channel_id=1, source_target_pairs={{0,8},{8,0},{1,9},{9,1},{2,10},{10,2},{3,11},{11,3},{4,12},{12,4},... | collective-permute-start | bytes 1769480 | tf_op jit(solution)/shard_map/ppermute | solution.py:776
  91.0 2.0 %collective-permute-done.4 = bf16[2304,128]{1,0:T(8,128)(2,1)S(1)} collective-permute-done((bf16[2304,128]{1,0:T(8,128)(2,1)S(1)}, bf16[2304,128]{1,0:T(8,128)(2,1)S(1)}, u32[]{:S(2)}, u32[]{:S(2)}) %collective-permute-start.4) | collective-permute-done | bytes 589856 | tf_op jit(solution)/shard_map/ppermute | solution.py:776
  93.0 0.2 add_convert_fusion
  93.2 18.1 %all_to_all.46 = bf16[16,144,128]{2,1,0:T(8,128)(2,1)S(1)} all-to-all(bf16[16,144,128]{2,1,0:T(8,128)(2,1)S(1)} %bitcast.38), channel_id=1, replica_groups=mesh['z_hi'=2,'x'=4,'y'=4,'core'=2,'section'=8] {'x','y'}, dimensions={0} | all-to-all | bytes 1179648 | tf_op jit(solution)/shard_map/all_to_all | solution.py:778
  111.3 0.1 shares.1
  111.4 8.2 %collective-permute-start.5 = (bf16[80,128]{1,0:T(8,128)(2,1)S(1)}, bf16[80,128]{1,0:T(8,128)(2,1)S(1)}, u32[]{:S(2)}, u32[]{:S(2)}) collective-permute-start(bf16[80,128]{1,0:T(8,128)(2,1)S(1)} %get-tuple-element.49), channel_id=1, source_target_pairs={{0,256},{256,0},{1,257},{257,1},{2,258},{258,2},{3,259},{259,3},{4... | collective-permute-start | bytes 61448 | tf_op jit(solution)/shard_map/ppermute | solution.py:781
  119.6 3.4 %input_grad.1 = bf16[1024,512]{1,0:T(8,128)(2,1)} custom-call(s32[2]{0:T(128)S(1)} %pad_add_fusion.where_ref, f32[64,128]{1,0:T(8,128)S(1)} %bitcast.35, bf16[1024,512]{1,0:T(8,128)(2,1)S(1)} %get-tuple-element.37.base_ref, bf16[1024,512]{1,0:T(8,128)(2,1)} %bitcast.37, bf16[1024,128]{1,0:T(8,128)(2,1)S(1)} %get-tuple-element.44.e_one_ref, ...), custom_call_target="tpu_custom_call" | custom-call | flops 200000000 | bytes 6000000 | tf_op jit(solution)/shard_map/input_grad/pallas_call | solution.py:567
  123.0 2.8 %collective-permute-done.5.got_ref = bf16[80,128]{1,0:T(8,128)(2,1)S(1)} collective-permute-done((bf16[80,128]{1,0:T(8,128)(2,1)S(1)}, bf16[80,128]{1,0:T(8,128)(2,1)S(1)}, u32[]{:S(2)}, u32[]{:S(2)}) %collective-permute-start.5) | collective-permute-done | bytes 20512 | tf_op jit(solution)/shard_map/ppermute | solution.py:781
  125.8 0.6 weight_grads.1
  (5 shorter events, 0.0 us)
Async XLA Ops:
  0.6 14.8 %collective-permute-start = (f32[32,128]{1,0:T(8,128)}, f32[32,128]{1,0:T(8,128)S(1)}, u32[]{:S(2)}, u32[]{:S(2)}) collective-permute-start(f32[32,128]{1,0:T(8,128)} %param.17), channel_id=1, source_target_pairs={{0,260},{1,261},{2,262},{3,263},{4,256},{5,257},{6,258},{7,259},{2... | collective-permute-start | bytes 49160 | tf_op jit(solution)/shard_map/ppermute | solution.py:697
  16.2 25.7 %copy-start.7 = (s32[32]{0:T(128)S(1)}, s32[32]{0:T(128)}, u32[]{:S(2)}) copy-start(s32[32]{0:T(128)} %param.18) | copy-start | bytes 388
  17.1 22.0 %all-to-all-start = ((f32[16,64,128]{2,1,0:T(8,128)}), f32[16,64,128]{2,1,0:T(8,128)S(1)}, u32[]{:S(2)}, u32[]{:S(2)}) async-start(f32[16,64,128]{2,1,0:T(8,128)} %bitcast.5), calls=%async_computation | async-start | bytes 1048576 | tf_op jit(solution)/shard_map/all_to_all | solution.py:717
  24.5 24.8 %copy-start = (bf16[512,256]{1,0:T(8,128)(2,1)S(1)}, bf16[512,256]{1,0:T(8,128)(2,1)}, u32[]{:S(2)}) copy-start(bf16[512,256]{1,0:T(8,128)(2,1)} %head_in_ref.1) | copy-start | bytes 786436
  24.5 24.8 %copy-start.1 = (bf16[256,128]{1,0:T(8,128)(2,1)S(1)}, bf16[256,128]{1,0:T(8,128)(2,1)}, u32[]{:S(2)}) copy-start(bf16[256,128]{1,0:T(8,128)(2,1)} %head_out_ref.1) | copy-start | bytes 196612
  24.5 24.8 %copy-start.3 = (bf16[2,256]{1,0:T(2,128)(2,1)S(1)}, bf16[2,256]{1,0:T(2,128)(2,1)}, u32[]{:S(2)}) copy-start(bf16[2,256]{1,0:T(2,128)(2,1)} %head_pre_ref.1) | copy-start | bytes 3076
  24.6 24.8 %copy-start.4 = (s32[1,32]{1,0:T(1,128)S(1)}, s32[1,32]{1,0:T(1,128)}, u32[]{:S(2)}) copy-start(s32[1,32]{1,0:T(1,128)} %plan_ref.1) | copy-start | bytes 388
  24.6 14.5 %collective-permute-start.1 = (bf16[72,128]{1,0:T(8,128)(2,1)S(1)}, bf16[72,128]{1,0:T(8,128)(2,1)S(1)}, u32[]{:S(2)}, u32[]{:S(2)}) collective-permute-start(bf16[72,128]{1,0:T(8,128)(2,1)S(1)} %pad_maximum_fusion.1), channel_id=1, source_target_pairs={{0,256},{256,0},{1,257},{257,1},{2,258},{258,2},{3,259},{259,3},{4... | collective-permute-start | bytes 55304 | tf_op jit(solution)/shard_map/ppermute | solution.py:718
  40.0 9.3 %collective-permute-start.2 = (f32[1024,128]{1,0:T(8,128)S(1)}, f32[1024,128]{1,0:T(8,128)S(1)}, u32[]{:S(2)}, u32[]{:S(2)}) collective-permute-start(f32[1024,128]{1,0:T(8,128)S(1)} %bitcast.32), channel_id=1, source_target_pairs={{0,8},{8,0},{1,9},{9,1},{2,10},{10,2},{3,11},{11,3},{4,12},{12,4},... | collective-permute-start | bytes 1572872 | tf_op jit(solution)/shard_map/ppermute | solution.py:725
  42.1 21.1 %all-to-all-start.1 = ((bf16[16,144,128]{2,1,0:T(8,128)(2,1)}), bf16[16,144,128]{2,1,0:T(8,128)(2,1)S(1)}, u32[]{:S(2)}, u32[]{:S(2)}) async-start(bf16[16,144,128]{2,1,0:T(8,128)(2,1)} %bitcast.11), calls=%async_computation.1 | async-start | bytes 1179648 | tf_op jit(solution)/shard_map/all_to_all | solution.py:735
  63.1 9.4 %collective-permute-start.3 = (bf16[2304,128]{1,0:T(8,128)(2,1)S(1)}, bf16[2304,128]{1,0:T(8,128)(2,1)S(1)}, u32[]{:S(2)}, u32[]{:S(2)}) collective-permute-start(bf16[2304,128]{1,0:T(8,128)(2,1)S(1)} %bitcast.29), channel_id=1, source_target_pairs={{0,8},{8,0},{1,9},{9,1},{2,10},{10,2},{3,11},{11,3},{4,12},{12,4},... | collective-permute-start | bytes 1769480 | tf_op jit(solution)/shard_map/ppermute | solution.py:750
  65.0 18.1 %all-to-all-start.2 = ((f32[8,8,128]{2,1,0:T(8,128)}), f32[8,8,128]{2,1,0:T(8,128)S(1)}, u32[]{:S(2)}, u32[]{:S(2)}) async-start(f32[8,8,128]{2,1,0:T(8,128)} %bitcast.13), calls=%async_computation.2 | async-start | bytes 65536 | tf_op jit(solution)/shard_map/all_to_all | solution.py:748
  73.5 9.6 %copy-start.2 = (f32[1,512]{1,0:T(1,128)S(1)}, f32[1,512]{1,0:T(1,128)}, u32[]{:S(2)}) copy-start(f32[1,512]{1,0:T(1,128)} %gain3_ref.1) | copy-start | bytes 6148
  73.5 9.6 %copy-start.5 = (f32[1,128]{1,0:T(1,128)S(1)}, f32[1,128]{1,0:T(1,128)}, u32[]{:S(2)}) copy-start(f32[1,128]{1,0:T(1,128)} %gain1_ref.1) | copy-start | bytes 1540
  73.6 9.6 %copy-start.6 = (f32[1,128]{1,0:T(1,128)S(1)}, f32[1,128]{1,0:T(1,128)}, u32[]{:S(2)}) copy-start(f32[1,128]{1,0:T(1,128)} %gain2_ref.1) | copy-start | bytes 1540
  89.1 3.9 %collective-permute-start.4 = (bf16[2304,128]{1,0:T(8,128)(2,1)S(1)}, bf16[2304,128]{1,0:T(8,128)(2,1)S(1)}, u32[]{:S(2)}, u32[]{:S(2)}) collective-permute-start(bf16[2304,128]{1,0:T(8,128)(2,1)S(1)} %get-tuple-element.47), channel_id=1, source_target_pairs={{0,8},{8,0},{1,9},{9,1},{2,10},{10,2},{3,11},{11,3},{4,12},{12,4},... | collective-permute-start | bytes 1769480 | tf_op jit(solution)/shard_map/ppermute | solution.py:776
  111.4 14.4 %collective-permute-start.5 = (bf16[80,128]{1,0:T(8,128)(2,1)S(1)}, bf16[80,128]{1,0:T(8,128)(2,1)S(1)}, u32[]{:S(2)}, u32[]{:S(2)}) collective-permute-start(bf16[80,128]{1,0:T(8,128)(2,1)S(1)} %get-tuple-element.49), channel_id=1, source_target_pairs={{0,256},{256,0},{1,257},{257,1},{2,258},{258,2},{3,259},{259,3},{4... | collective-permute-start | bytes 61448 | tf_op jit(solution)/shard_map/ppermute | solution.py:781
